TPU v7x, 256 devices: a whole 4x4x8 slice. The times are simulated.
256 devices in a mesh: blk: 32 (over x_hi, z, core), feat: 8 (over x_lo, y).
Axes of the slice: x: 4 (x_hi: 2, x_lo: 2; x = x_hi * 2 + x_lo), y: 4, z: 8, core: 2. Of those that a mesh axis runs over, the one named last changes fastest.
Arguments:
- pool_embed: bfloat16 [262144, 1536], P('blk', 'feat'), may hold values from -16 to 16
- label_embed: bfloat16 [2048, 1536], P('blk', 'feat'), may hold values from -4 to 4
- label_class: int32 [2048], P('blk'), may hold values from 0 to 999
Outputs:
- log_probs: float32 [262144, 1000], P(('blk', 'feat'))
- entropy: float32 [262144], P(('blk', 'feat'))
All inputs are finite; a program needn't handle non-finite values.
Results may differ from a plain program's by a relative error of at most 0.0009.
Values may be sent and summed in bfloat16 or wider, within the bound.
No kernel may reach another device: no remote copies, remote signals or barrier semaphores. Data moves between devices by JAX's collectives and lax.ppermute only.
A program may use at most 64 MiB of HBM per device.

v0:
```python
import math
import jax
import jax.numpy as jnp
from jax import lax
from jax.sharding import PartitionSpec as P

C = 1000
SMOOTHING = 0.1


def per_device(pool_embed, label_embed, label_class):
    pool_rows = lax.all_to_all(pool_embed, "feat", split_axis=0, concat_axis=1, tiled=True)
    key_rows = lax.all_gather(label_embed, "feat", axis=1, tiled=True)
    width = pool_rows.shape[1]
    scale = 2.0 / math.sqrt(width)
    count = pool_rows.shape[0]
    class_ids = jnp.arange(C, dtype=jnp.int32)
    run_max = jnp.full((count,), -1e30, jnp.float32)
    key_piece = lax.all_gather(key_rows, "blk", axis=0, tiled=True)
    class_piece = lax.all_gather(label_class, "blk", axis=0, tiled=True)
    scores = (
        lax.dot_general(
            pool_rows, key_piece, (((1,), (1,)), ((), ())), preferred_element_type=jnp.float32
        )
        * scale
    )
    new_max = jnp.maximum(run_max, jnp.max(scores, axis=1))
    weights = jnp.exp(scores - new_max[:, None])
    onehot = (class_piece[:, None] == class_ids[None, :]).astype(jnp.bfloat16)
    weight_sum = jnp.sum(weights, axis=1)
    class_mass = jnp.dot(weights.astype(jnp.bfloat16), onehot, preferred_element_type=jnp.float32)
    final = (new_max, weight_sum, class_mass)
    run_max, weight_sum, class_mass = final
    probability = (1.0 - SMOOTHING) * class_mass / weight_sum[:, None] + SMOOTHING / C
    log_probs = jnp.log(probability)
    entropy = -jnp.sum(probability * log_probs, axis=1)
    return (log_probs, entropy)


def solution(mesh):
    placed = (P("blk", "feat"), P("blk", "feat"), P("blk"))
    return jax.shard_map(
        per_device,
        mesh=mesh,
        in_specs=placed,
        out_specs=(P(("blk", "feat"), None), P(("blk", "feat"))),
        check_vma=False,
    )
```

profile of v0, /device:TPU:1, one launch (start us, length us, event | category | flops | bytes accessed | tf_op | source)
XLA Modules:
  0.0 162.0 jit_solution(10843462604677200588)
XLA Ops:
  7.2 0.0 all-gather.3.cloned.1.call-start
  7.2 24.1 %all-gather = bf16[8,192,64]{1,2,0:T(8,128)(2,1)S(1)} all-gather(bf16[1,192,64]{1,2,0:T(8,128)(2,1)} %bitcast.19), channel_id=1, replica_groups=mesh['blk'=32,'feat'=8] {'feat'}, dimensions={0}, use_global_device_ids=true | all-gather | bytes 221184 | tf_op jit(solution)/shard_map/all_gather | solution.py:13
  31.3 0.1 copy.9
  31.4 0.9 reshape.16
  32.3 0.0 all-gather.3.cloned.1.call-update
  32.3 0.0 copy-start.1
  32.4 0.0 copy-start
  32.4 4.0 %copy.12 = bf16[24,8,8,1024]{3,2,0,1:T(8,128)(2,1)} copy(bf16[24,8,8,1024]{3,2,1,0:T(8,128)(2,1)} %bitcast.16) | data formatting | bytes 6291456 | tf_op jit(solution)/shard_map/all_to_all | solution.py:12
  36.4 4.4 %all-to-all-start = ((bf16[8,1024,192]{1,2,0:T(8,128)(2,1)}), bf16[8,1024,192]{1,2,0:T(8,128)(2,1)S(1)}, u32[]{:S(2)}, u32[]{:S(2)}) async-start(bf16[8,1024,192]{1,2,0:T(8,128)(2,1)} %bitcast.15), calls=%async_computation | async-start | bytes 6291456 | tf_op jit(solution)/shard_map/all_to_all | solution.py:12
  40.7 0.0 copy-done.1
  40.7 0.6 dynamic-slice
  42.0 0.0 copy-done
  42.0 0.3 dynamic-update-slice
  42.3 30.7 %all-reduce = s32[2048]{0:T(1024)S(1)} all-reduce(s32[2048]{0:T(1024)S(1)} %dynamic-update-slice), channel_id=1, replica_groups=mesh['blk'=32,'feat'=8] {'blk'}, use_global_device_ids=true, to_apply=%add | all-reduce | flops 2048 | bytes 16384
  73.0 0.4 all-to-all-done
  73.4 62.5 %all-gather.3.cloned.1.call-done = bf16[2048,1536]{1,0:T(8,128)(2,1)} async-done(((bf16[64,1536]{1,0:T(8,128)(2,1)}), bf16[2048,1536]{1,0:T(8,128)(2,1)}) %all-gather.3.cloned.1.call-update) | async-done | bytes 6291472 | tf_op jit(solution)/shard_map/all_gather | solution.py:19
  135.9 9.0 %multiply_reduce_fusion = (f32[1024]{0:T(1024)S(1)}, f32[1024,2048]{1,0:T(8,128)S(1)}) fusion(bf16[1024,1536]{0,1:T(8,128)(2,1)S(1)} %bitcast.17, bf16[2048,1536]{1,0:T(8,128)(2,1)} %all-gather.3.cloned.1.call-done), kind=kOutput, calls=%fused_computation.3 | convolution fusion | flops 6446644224 | bytes 17829888 | tf_op jit(solution)/shard_map/dot_general | solution.py:22
  144.9 1.9 %fusion.1 = f32[1024]{0:T(1024)S(1)} fusion(f32[1024,2048]{1,0:T(8,128)S(1)} %get-tuple-element.5, f32[1024]{0:T(1024)S(1)} %broadcast_maximum_fusion), kind=kLoop, calls=%fused_computation.4 | loop fusion | flops 6290432 | bytes 8396800 | tf_op jit(solution)/shard_map/reduce_sum | solution.py:30
  146.8 7.8 %multiply_reduce_fusion.1 = (f32[1024]{0:T(1024)S(1)}, f32[1024,1000]{0,1:T(8,128)}) fusion(f32[1024]{0:T(1024)S(1)} %fusion.1, s32[2048]{0:T(1024)S(1)} %all-reduce, f32[1024,2048]{1,0:T(8,128)S(1)} %get-tuple-element.5, f32[1024]{0:T(1024)S(1)} %broadcast_maximum_fusion), kind=kOutput, calls=%fused_computation.9 | convolution fusion | flops 4207762432 | bytes 12505088 | tf_op jit(solution)/shard_map/dot_general | solution.py:31
  154.6 0.6 neg.3
  (2 shorter events, 0.0 us)
Async XLA Ops:
  7.2 128.7 %all-gather.3.cloned.1.call-start = ((), (), s32[]{:S(2)}) async-start(), calls=%async_computation.1 | async-start | bytes 6488064 | tf_op jit(solution)/shard_map/all_gather | solution.py:19
  32.3 8.4 %copy-start.1 = (u32[256]{0:T(256)S(1)}, u32[256]{0:T(256)}, u32[]{:S(2)}) copy-start(u32[256]{0:T(256)} %constant.14) | copy-start | bytes 3076
  32.4 9.6 %copy-start = (s32[64]{0:T(128)S(1)}, s32[64]{0:T(128)}, u32[]{:S(2)}) copy-start(s32[64]{0:T(128)} %param.5) | copy-start | bytes 772
  36.4 37.0 %all-to-all-start = ((bf16[8,1024,192]{1,2,0:T(8,128)(2,1)}), bf16[8,1024,192]{1,2,0:T(8,128)(2,1)S(1)}, u32[]{:S(2)}, u32[]{:S(2)}) async-start(bf16[8,1024,192]{1,2,0:T(8,128)(2,1)} %bitcast.15), calls=%async_computation | async-start | bytes 6291456 | tf_op jit(solution)/shard_map/all_to_all | solution.py:12
Sparse Core Ops, SparseCore 0:
  32.5 103.3 all-gather.2
where the time goes:
time: 162 us
  waiting for transfers between devices  62.9 us (39%)
  blocking collectives  54.7 us (34%)
  matrix products  16.7 us (10%)
  between operations  14.7 us (9%)
  local copies, waits for them, and re-layouts  5.93 us (4%)
  starting transfers between devices  4.41 us (3%)
  other arithmetic  2.53 us (2%)
    all_gather x1, waiting for transfers between devices, per_device(): key_piece = lax.all_gather(key_rows, 'blk', axis=0, tiled=True)  62.5 us
    unnamed x1, blocking collectives  30.7 us
    all_gather x1, blocking collectives, per_device(): key_rows = lax.all_gather(label_embed, 'feat', axis=1, tiled=True)  24.1 us
    dot_general x1, matrix products, per_device(): lax.dot_general(pool_rows, key_piece, (((1,), (1,)), ((), ())), preferred...  8.99 us
    dot_general x1, matrix products, per_device(): jnp.dot(weights.astype(jnp.bfloat16), onehot, preferred_element_type=jnp....  7.75 us
    all_to_all x1, starting transfers between devices, per_device(): lax.all_to_all(pool_embed, 'feat', split_axis=0, concat_axis=1, tiled=True)  4.37 us
    all_to_all x1, local copies, waits for them, and re-layouts, per_device(): lax.all_to_all(pool_embed, 'feat', split_axis=0, concat_axis=1, tiled=True)  4 us
  transfers between devices with their start and end apart: 2, of which 2 were waited for; matrix products, arithmetic and copies ran while one was open for 3% of the time, Pallas kernels for 0%

commit v1 on v0

--- a/solution.py
+++ b/solution.py
@@ -16,7 +16,9 @@
     count = pool_rows.shape[0]
     class_ids = jnp.arange(C, dtype=jnp.int32)
     run_max = jnp.full((count,), -1e30, jnp.float32)
-    key_piece = lax.all_gather(key_rows, "blk", axis=0, tiled=True)
+    key_piece = jnp.concatenate(
+        lax.all_to_all(jnp.stack([key_rows] * lax.axis_size("blk")), "blk", 0, 0), axis=0
+    )
     class_piece = lax.all_gather(label_class, "blk", axis=0, tiled=True)
     scores = (
         lax.dot_general(

time: 162 us -> 258 us (1.59)
  blocking collectives: 54.7 us -> 203 us
  waiting for transfers between devices: 62.9 us -> 0.01 us
  starting transfers between devices: 4.41 us -> 24.3 us
  between operations: 14.7 us -> 1.37 us
  local copies, waits for them, and re-layouts: 5.93 us -> 10.2 us
    unnamed x1, blocking collectives: 30.7 us -> 148 us
    all_gather x1 -> x0, waiting for transfers between devices: 62.5 us -> none  [per_device(): key_piece = lax.all_gather(key_rows, 'blk', axis=0, tiled=True)]
    all_gather x1, blocking collectives: 24.1 us -> 54.6 us  [per_device(): key_rows = lax.all_gather(label_embed, 'feat', axis=1, tiled=True)]
    all_to_all x0 -> x1, starting transfers between devices: none -> 18.4 us  [per_device(): lax.all_to_all(jnp.stack([key_rows] * lax.axis_size('blk')), 'blk', 0, 0)]
    another operation x0 -> x1, local copies, waits for them, and re-layouts: none -> 4.3 us  [per_device(): jnp.stack([key_rows] * lax.axis_size('blk'))]
  transfers between devices with their start and end apart: 2 -> 2, of which waited for: 2 -> 0; matrix products, arithmetic and copies ran while one was open for 3% -> 1% of each run, Pallas kernels for 0% -> 0%
where the time goes in v1:
time: 258 us
  blocking collectives  203 us (79%)
  starting transfers between devices  24.3 us (9%)
  matrix products  16.8 us (7%)
  local copies, waits for them, and re-layouts  10.2 us (4%)
    unnamed x1, blocking collectives  148 us
    all_gather x1, blocking collectives, per_device(): key_rows = lax.all_gather(label_embed, 'feat', axis=1, tiled=True)  54.6 us
    all_to_all x1, starting transfers between devices, per_device(): lax.all_to_all(jnp.stack([key_rows] * lax.axis_size('blk')), 'blk', 0, 0)  18.4 us
    dot_general x1, matrix products, per_device(): lax.dot_general(pool_rows, key_piece, (((1,), (1,)), ((), ())), preferred...  8.99 us
    dot_general x1, matrix products, per_device(): jnp.dot(weights.astype(jnp.bfloat16), onehot, preferred_element_type=jnp....  7.76 us
    all_to_all x1, starting transfers between devices, per_device(): lax.all_to_all(pool_embed, 'feat', split_axis=0, concat_axis=1, tiled=True)  5.95 us
  transfers between devices with their start and end apart: 2, of which 0 were waited for; matrix products, arithmetic and copies ran while one was open for 1% of the time, Pallas kernels for 0%

profile of v1, /device:TPU:1, one launch (start us, length us, event | category | flops | bytes accessed | tf_op | source)
XLA Modules:
  0.0 257.9 jit_solution(3565275770060017201)
XLA Ops:
  0.6 0.0 copy-start
  0.6 4.0 %copy.13 = bf16[24,8,8,1024]{3,2,0,1:T(8,128)(2,1)} copy(bf16[24,8,8,1024]{3,2,1,0:T(8,128)(2,1)} %bitcast.17) | data formatting | bytes 6291456 | tf_op jit(solution)/shard_map/all_to_all | solution.py:12
  4.6 5.9 %all-to-all-start = ((bf16[8,1024,192]{1,2,0:T(8,128)(2,1)}), bf16[8,1024,192]{1,2,0:T(8,128)(2,1)S(1)}, u32[]{:S(2)}, u32[]{:S(2)}) async-start(bf16[8,1024,192]{1,2,0:T(8,128)(2,1)} %bitcast.16), calls=%async_computation | async-start | bytes 6291456 | tf_op jit(solution)/shard_map/all_to_all | solution.py:12
  10.6 0.0 copy-done
  10.6 54.6 %all-gather = bf16[8,192,64]{1,2,0:T(8,128)(2,1)S(1)} all-gather(bf16[1,192,64]{1,2,0:T(8,128)(2,1)S(1)} %bitcast.20), channel_id=1, replica_groups=mesh['blk'=32,'feat'=8] {'feat'}, dimensions={0}, use_global_device_ids=true | all-gather | bytes 221184 | tf_op jit(solution)/shard_map/all_gather | solution.py:13
  65.1 0.1 copy.10
  65.3 0.9 reshape.22
  66.2 0.0 all-to-all-done
  66.2 4.3 %stack.2 = bf16[32,64,1536]{2,1,0:T(8,128)(2,1)} broadcast(bf16[64,1536]{1,0:T(8,128)(2,1)} %bitcast.19), dimensions={1,2} | broadcast | bytes 6488064 | tf_op jit(solution)/shard_map/stack | solution.py:20
  70.5 0.0 copy-start.2
  70.5 0.0 copy-start.1
  70.5 18.4 %all-to-all-start.1 = ((bf16[32,64,1536]{2,1,0:T(8,128)(2,1)}), bf16[32,64,1536]{2,1,0:T(8,128)(2,1)}, u32[]{:S(2)}, u32[]{:S(2)}) async-start(bf16[32,64,1536]{2,1,0:T(8,128)(2,1)} %stack.2), calls=%async_computation.1 | async-start | bytes 12582912 | tf_op jit(solution)/shard_map/all_to_all | solution.py:20
  88.9 0.0 copy-done.2
  88.9 0.6 dynamic-slice
  90.2 0.0 copy-done.1
  90.2 0.3 dynamic-update-slice
  90.5 148.1 %all-reduce = s32[2048]{0:T(1024)S(1)} all-reduce(s32[2048]{0:T(1024)S(1)} %dynamic-update-slice), channel_id=1, replica_groups=mesh['blk'=32,'feat'=8] {'blk'}, use_global_device_ids=true, to_apply=%add | all-reduce | flops 2048 | bytes 16384
  238.6 0.0 all-to-all-done.1
  238.6 9.0 %multiply_reduce_fusion = (f32[1024]{0:T(1024)S(1)}, f32[1024,2048]{1,0:T(8,128)S(1)}) fusion(bf16[1024,1536]{0,1:T(8,128)(2,1)S(1)} %bitcast.18, bf16[2048,1536]{1,0:T(8,128)(2,1)} %bitcast.5), kind=kOutput, calls=%fused_computation.3 | convolution fusion | flops 6446644224 | bytes 17829888 | tf_op jit(solution)/shard_map/dot_general | solution.py:24
  247.6 1.9 fusion.1
  249.5 7.8 %multiply_reduce_fusion.1 = (f32[1024]{0:T(1024)S(1)}, f32[1024,1000]{0,1:T(8,128)}) fusion(f32[1024]{0:T(1024)S(1)} %fusion.1, s32[2048]{0:T(1024)S(1)} %all-reduce, f32[1024,2048]{1,0:T(8,128)S(1)} %get-tuple-element.5, f32[1024]{0:T(1024)S(1)} %broadcast_maximum_fusion), kind=kOutput, calls=%fused_computation.9 | convolution fusion | flops 4207762432 | bytes 12505088 | tf_op jit(solution)/shard_map/dot_general | solution.py:33
  257.3 0.6 neg.3
  (2 shorter events, 0.0 us)
Async XLA Ops:
  0.6 10.0 %copy-start = (bf16[64,192]{1,0:T(8,128)(2,1)S(1)}, bf16[64,192]{1,0:T(8,128)(2,1)}, u32[]{:S(2)}) copy-start(bf16[64,192]{1,0:T(8,128)(2,1)} %param.4) | copy-start | bytes 73732
  4.6 61.6 %all-to-all-start = ((bf16[8,1024,192]{1,2,0:T(8,128)(2,1)}), bf16[8,1024,192]{1,2,0:T(8,128)(2,1)S(1)}, u32[]{:S(2)}, u32[]{:S(2)}) async-start(bf16[8,1024,192]{1,2,0:T(8,128)(2,1)} %bitcast.16), calls=%async_computation | async-start | bytes 6291456 | tf_op jit(solution)/shard_map/all_to_all | solution.py:12
  70.5 18.4 %copy-start.2 = (u32[256]{0:T(256)S(1)}, u32[256]{0:T(256)}, u32[]{:S(2)}) copy-start(u32[256]{0:T(256)} %constant.14) | copy-start | bytes 3076
  70.5 19.7 %copy-start.1 = (s32[64]{0:T(128)S(1)}, s32[64]{0:T(128)}, u32[]{:S(2)}) copy-start(s32[64]{0:T(128)} %param.5) | copy-start | bytes 772
  70.5 168.1 %all-to-all-start.1 = ((bf16[32,64,1536]{2,1,0:T(8,128)(2,1)}), bf16[32,64,1536]{2,1,0:T(8,128)(2,1)}, u32[]{:S(2)}, u32[]{:S(2)}) async-start(bf16[32,64,1536]{2,1,0:T(8,128)(2,1)} %stack.2), calls=%async_computation.1 | async-start | bytes 12582912 | tf_op jit(solution)/shard_map/all_to_all | solution.py:20
